TPU v7x, 32 devices: a whole 2x2x4 slice. The times are simulated.
32 devices in a mesh: chan: 8 (over y, x, core), win: 4 (over z).
Axes of the slice: x: 2, y: 2, z: 4, core: 2. Of those that a mesh axis runs over, the one named last changes fastest.
Arguments:
- spectra: float32 [4, 256, 2, 4096], P('win', 'chan'), may hold values from -2000 to 2000
- sources: int32 [2, 8], replicated, may hold values from 0 to 255, as said below
- window_valid: int32 [4, 256], P('win', 'chan'), may hold values 0 or 1
Outputs:
- correlations: float32 [2, 8, 256, 256], P(None, 'win', 'chan')
Inputs may be any that keep to these rules, and one draw needn't show every extreme that they name: sources[t, s] is a channel of owner s, that is between (s) * 32 and (s + 1) * 32 - 1; the entries of one turn are distinct.
All inputs are finite; a program needn't handle non-finite values. No bound on the sum of `window_valid` on one device may be relied on, other than what follows from the above.
Results may differ from a plain program's by a relative error of at most 0.0022.
Values may be sent and summed in bfloat16 or wider, within the bound.
A program may use at most 64 MiB of HBM per device.

v0:
```python
import math
import jax
import jax.numpy as jnp
from jax import lax
from jax.sharding import PartitionSpec as P

LAGS = 256


def whiten(spectra, window_valid):
    mean_power = jnp.mean(spectra * spectra, axis=(2, 3), keepdims=True)
    valid_flags = window_valid.astype(jnp.float32)[:, :, None, None]
    whitened = valid_flags * spectra / jnp.sqrt(mean_power + 1e-05)
    return whitened.astype(jnp.bfloat16).reshape(
        spectra.shape[0], spectra.shape[1], 2 * spectra.shape[3]
    )


def build_table(freq_count, lag_count):
    shifts = jnp.arange(lag_count, dtype=jnp.int32) - lag_count // 2
    freq_bins = jnp.arange(freq_count, dtype=jnp.int32)
    phase_index = freq_bins[:, None] * shifts[None, :] % (2 * freq_count)
    angles = phase_index.astype(jnp.float32) * (math.pi / freq_count)
    return jnp.concatenate([jnp.cos(angles), -jnp.sin(angles)], axis=0).astype(jnp.bfloat16)


def cross_block(source_piece, receivers, trig_table):
    half_width = receivers.shape[2] // 2
    src_real = source_piece[:, :, None, :half_width].astype(jnp.float32)
    src_imag = source_piece[:, :, None, half_width:].astype(jnp.float32)
    rec_real = receivers[:, None, :, :half_width].astype(jnp.float32)
    rec_imag = receivers[:, None, :, half_width:].astype(jnp.float32)
    cross_real = (src_real * rec_real + src_imag * rec_imag).astype(jnp.bfloat16)
    cross_imag = (src_imag * rec_real - src_real * rec_imag).astype(jnp.bfloat16)
    cross_both = jnp.concatenate([cross_real, cross_imag], axis=-1)
    lag_values = jnp.dot(
        cross_both.reshape(-1, 2 * half_width), trig_table, preferred_element_type=jnp.float32
    )
    lag_values = lag_values.reshape(
        source_piece.shape[0], source_piece.shape[1], receivers.shape[1], -1
    )
    return jnp.sum(lag_values, axis=0)


def local(spectra, sources, window_valid):
    whitened = whiten(spectra, window_valid)
    win_local = whitened.shape[0]
    chan_local = whitened.shape[1]
    freq_count = spectra.shape[3]
    turn_count = sources.shape[0]
    trig_table = build_table(freq_count, LAGS)
    norm_scale = 1.0 / math.sqrt(freq_count * win_local * lax.axis_size("win"))
    own_count = sources.shape[1] // lax.axis_size("chan")
    owner_index = lax.axis_index("chan")
    local_rows = (
        lax.dynamic_slice_in_dim(sources, owner_index * own_count, own_count, 1)
        - owner_index * chan_local
    )
    picked = jnp.take(whitened, local_rows.reshape(-1), axis=1).reshape(
        win_local, turn_count, own_count, 2 * freq_count
    )
    everything = lax.all_gather(picked, "chan", axis=2, tiled=True)
    per_turn = [everything[:, turn_index] for turn_index in range(turn_count)]
    results = []
    for gathered in per_turn:
        share_rows = gathered.shape[1] // lax.axis_size("win")

        def stack_term(first_row, row_count, gathered=gathered):
            sub_size = math.gcd(row_count, 8)
            sub_number = row_count // sub_size
            sub_blocks = gathered.reshape(
                win_local, sub_number, sub_size, 2 * freq_count
            ).transpose(1, 0, 2, 3)
            partial_value = lax.map(
                lambda source_piece: cross_block(source_piece, whitened, trig_table), sub_blocks
            )
            return partial_value.reshape(row_count, chan_local, -1)

        stacked = lax.psum_scatter(
            stack_term(jnp.int32(0), share_rows * lax.axis_size("win")),
            "win",
            scatter_dimension=0,
            tiled=True,
        )
        results.append(stacked * norm_scale)
    return jnp.stack(results, axis=0)


def solution(mesh):
    placed = (P("win", "chan", None, None), P(), P("win", "chan"))
    return jax.shard_map(
        local, mesh=mesh, in_specs=placed, out_specs=P(None, "win", "chan", None), check_vma=False
    )
```

profile of v0, /device:TPU:0, one launch (start us, length us, event | category | flops | bytes accessed | tf_op | source)
XLA Modules:
  0.0 96.3 jit_solution(6179811309796717721)
XLA Ops:
  6.5 0.0 reduce-scatter.3.cloned.1.call-start
  6.5 0.9 and_reduce_fusion
  7.4 0.1 reduce.2
  7.5 1.9 %multiply_reduce_fusion = f32[32]{0:T(128)S(1)} fusion(f32[1,32,2,4096]{3,2,1,0:T(2,128)} %param.3), kind=kLoop, calls=%fused_computation.25 | loop fusion | flops 524256 | bytes 1048704 | tf_op jit(solution)/shard_map/reduce_sum | solution.py:11
  9.4 0.7 convert_bitcast_fusion
  10.1 1.9 %fusion.12 = bf16[1,32,2,4096]{3,2,1,0:T(2,128)(2,1)S(1)} fusion(f32[1,32,2,4096]{3,2,1,0:T(2,128)} %param.3, f32[32]{0:T(128)S(1)} %add_sqrt_fusion, f32[32]{0:T(128)S(1)} %convert_bitcast_fusion), kind=kLoop, calls=%fused_computation.27 | loop fusion | flops 786432 | bytes 1573120 | tf_op jit(solution)/shard_map/convert_element_type | solution.py:14
  12.0 0.4 reshape.261
  12.4 0.3 copy.9
  12.7 0.6 gather_fusion
  13.3 0.1 fusion.19
  13.4 10.8 %all_gather.3 = bf16[1,2,8,8192]{3,1,0,2:T(2,128)(2,1)S(1)} all-gather(bf16[1,2,1,8192]{3,1,0,2:T(2,128)(2,1)S(1)} %fusion.19), channel_id=1, replica_groups=mesh['chan'=8,'win'=4] {'chan'}, dimensions={2}, use_global_device_ids=true | all-gather | bytes 294912 | tf_op jit(solution)/shard_map/all_gather | solution.py:62
  24.2 0.5 fusion.22
  24.6 0.3 copy_bitcast_fusion
  25.0 0.1 fusion.14
  25.1 17.0 %cosine_convert_fusion = (bf16[4096,256]{1,0:T(8,128)(2,1)S(1)}, bf16[4096,256]{1,0:T(8,128)(2,1)S(1)}) fusion(s32[256]{0:T(256)S(1)} %iota_add_fusion), kind=kLoop, calls=%fused_computation.19 | loop fusion | flops 17825792 | bytes 4195328 | tf_op jit(solution)/shard_map/convert.6
  42.0 0.0 copy-start
  42.1 0.0 copy-start.1
  42.1 3.5 %add_convert_fusion.1 = (bf16[1,8,32,4096]{3,2,1,0:T(8,128)(2,1)S(1)}, bf16[1,8,32,4096]{3,2,1,0:T(8,128)(2,1)S(1)}, bf16[1,8,32,4096]{3,2,1,0:T(8,128)(2,1)S(1)}, bf16[1,8,32,4096]{3,2,1,0:T(8,128)(2,1)}) fusion(f32[32,4096]{1,0:T(8,128)S(1)} %get-tuple-element.44, f32[8,4096]{1,0:T(8,128)S(1)} %get-tuple-element.48, f32[32,4096]{1,0:T(8,128)S(1)} %get-tuple-element.42, ...), kind=kLoop, calls=%fused_computation.23 | loop fusion | flops 16777216 | bytes 9961472 | tf_op jit(solution)/shard_map/while/body/eval_jaxpr/convert_element_type | solution.py:33
  45.6 0.0 copy-done
  45.6 0.0 copy-done.1
  45.6 1.9 %fusion.3 = f32[8,32,256]{2,1,0:T(8,128)} fusion(bf16[1,8,32,4096]{3,2,1,0:T(8,128)(2,1)S(1)} %get-tuple-element.31, bf16[1,8,32,4096]{3,2,1,0:T(8,128)(2,1)S(1)} %get-tuple-element.30, bf16[4096,256]{1,0:T(8,128)(2,1)S(1)} %get-tuple-element.52, bf16[4096,256]{1,0:T(8,128)(2,1)S(1)} %get-tuple-element.51), kind=kOutput, calls=%fused_computation.8 | convolution fusion | flops 1090519040 | bytes 8650752 | tf_op jit(solution)/shard_map/while/body/eval_jaxpr/dot_general | solution.py:36
  47.5 0.0 reduce-scatter.3.cloned.1.call-update
  47.6 0.0 reduce-scatter.5.cloned.1.call-start
  47.6 4.8 %fusion.6 = f32[8,32,256]{2,1,0:T(8,128)} fusion(bf16[1,8,32,4096]{3,2,1,0:T(8,128)(2,1)S(1)} %get-tuple-element.34, bf16[1,8,32,4096]{3,2,1,0:T(8,128)(2,1)} %get-tuple-element.40, bf16[4096,256]{1,0:T(8,128)(2,1)} %copy-done.1, bf16[4096,256]{1,0:T(8,128)(2,1)} %copy-done), kind=kOutput, calls=%fused_computation.13 | convolution fusion | flops 1090519040 | bytes 8650752 | tf_op jit(solution)/shard_map/while/body/eval_jaxpr/dot_general | solution.py:36
  52.4 0.0 reduce-scatter.5.cloned.1.call-update
  52.5 15.2 %reduce-scatter.3.cloned.1.call-done = f32[2,32,256]{2,1,0:T(8,128)} async-done(((f32[8,32,256]{2,1,0:T(8,128)}), f32[2,32,256]{2,1,0:T(8,128)}) %reduce-scatter.3.cloned.1.call-update) | async-done | bytes 65552 | tf_op jit(solution)/shard_map/reduce_scatter | solution.py:79
  67.6 0.8 multiply_bitcast_fusion.1
  68.5 19.5 %reduce-scatter.5.cloned.1.call-done = f32[2,32,256]{2,1,0:T(8,128)} async-done(((f32[8,32,256]{2,1,0:T(8,128)}), f32[2,32,256]{2,1,0:T(8,128)}) %reduce-scatter.5.cloned.1.call-update) | async-done | bytes 65552 | tf_op jit(solution)/shard_map/reduce_scatter | solution.py:79
  87.9 0.8 multiply_bitcast_fusion
  88.8 0.7 pad_maximum_fusion
  (5 shorter events, 0.1 us)
Async XLA Ops:
  6.5 61.1 %reduce-scatter.3.cloned.1.call-start = ((), (), s32[]{:S(2)}) async-start(), calls=%async_computation.2 | async-start | bytes 327680 | tf_op jit(solution)/shard_map/reduce_scatter | solution.py:79
  42.0 3.5 %copy-start = (bf16[4096,256]{1,0:T(8,128)(2,1)}, bf16[4096,256]{1,0:T(8,128)(2,1)S(1)}, u32[]{:S(2)}) copy-start(bf16[4096,256]{1,0:T(8,128)(2,1)S(1)} %get-tuple-element.51) | copy-start | bytes 6291460
  42.1 3.5 %copy-start.1 = (bf16[4096,256]{1,0:T(8,128)(2,1)}, bf16[4096,256]{1,0:T(8,128)(2,1)S(1)}, u32[]{:S(2)}) copy-start(bf16[4096,256]{1,0:T(8,128)(2,1)S(1)} %get-tuple-element.52) | copy-start | bytes 6291460
  47.6 40.4 %reduce-scatter.5.cloned.1.call-start = ((), (), s32[]{:S(2)}) async-start(), calls=%async_computation.3 | async-start | bytes 327680 | tf_op jit(solution)/shard_map/reduce_scatter | solution.py:79
Sparse Core Ops, SparseCore 0:
  47.7 19.8 reduce-scatter.2
  70.0 17.9 reduce-scatter.4
where the time goes:
time: 96.6 us; the launch traced here: 96.3 us
  waiting for transfers between devices  34.7 us (36%)
  other arithmetic  28.5 us (30%)
  between operations  13.5 us (14%)
  blocking collectives  10.8 us (11%)
  matrix products  6.77 us (7%)
  local copies, waits for them, and re-layouts  2.06 us (2%)
    reduce_scatter x2, waiting for transfers between devices, local(): lax.psum_scatter(stack_term(jnp.int32(0), share_rows * lax.axis_size('win...  34.6 us
    another operation x1, other arithmetic  17 us
    all_gather x1, blocking collectives, local(): everything = lax.all_gather(picked, 'chan', axis=2, tiled=True)  10.8 us
    dot_general x2, matrix products, cross_block(): jnp.dot(cross_both.reshape(-1, 2 * half_width), trig_table, preferred_ele...  6.77 us
    convert_element_type x1, other arithmetic, cross_block(): (src_real * rec_real + src_imag * rec_imag).astype(jnp.bfloat16)  3.51 us
    another operation x3, other arithmetic, local(): return jnp.stack(results, axis=0)  2.35 us
  transfers between devices with their start and end apart: 2, of which 2 were waited for; matrix products, arithmetic and copies ran while one was open for 6% of the time, Pallas kernels for 0%

commit v1 on v0

--- a/solution.py
+++ b/solution.py
@@ -59,7 +59,34 @@
     picked = jnp.take(whitened, local_rows.reshape(-1), axis=1).reshape(
         win_local, turn_count, own_count, 2 * freq_count
     )
-    everything = lax.all_gather(picked, "chan", axis=2, tiled=True)
+    plain, carry_out, d_next = (
+        jax.lax.axis_size("chan"),
+        jax.lax.axis_index("chan"),
+        picked.shape[2],
+    )
+    copies = []
+    for q, d in enumerate(picked.shape):
+        copies.append(d * plain if q == 2 else d)
+    everything = lax.dynamic_update_slice_in_dim(
+        jnp.zeros(copies, picked.dtype), picked, carry_out * d_next, axis=2
+    )
+    after = latest = picked
+    for pp in tuple(range(1, plain // 2 + 1)):
+        in_order = []
+        for q in tuple(range(plain)):
+            in_order.append((q, (q + 1) % plain))
+        after = jax.lax.ppermute(after, "chan", in_order)
+        everything = lax.dynamic_update_slice_in_dim(
+            everything, after, (carry_out - pp) % plain * d_next, axis=2
+        )
+        if 2 * pp < plain:
+            blocks_here = []
+            for q in tuple(range(plain)):
+                blocks_here.append((q, (q - 1) % plain))
+            latest = jax.lax.ppermute(latest, "chan", blocks_here)
+            everything = lax.dynamic_update_slice_in_dim(
+                everything, latest, (carry_out + pp) % plain * d_next, axis=2
+            )
     per_turn = [everything[:, turn_index] for turn_index in range(turn_count)]
     results = []
     for gathered in per_turn:

time: 96.6 us -> 109 us (1.13)
  blocking collectives: 10.8 us -> 0 us
  starting transfers between devices: 0.04 us -> 8.72 us
  local copies, waits for them, and re-layouts: 2.06 us -> 9.89 us
  waiting for transfers between devices: 34.7 us -> 40.1 us
  other arithmetic: 28.5 us -> 29.8 us
    all_gather x1 -> x0, blocking collectives: 10.8 us -> none  [local(): everything = lax.all_gather(picked, 'chan', axis=2, tiled=True)]
    ppermute x0 -> x7, starting transfers between devices: none -> 8.67 us  [the longest x3 8.16 us: local(): latest = jax.lax.ppermute(latest, 'chan', blocks_here)]
    dynamic_update_slice x0 -> x8, local copies, waits for them, and re-layouts: none -> 8.13 us  [the longest x4 4.07 us: local(): lax.dynamic_update_slice_in_dim(everything, after, (carry_out - pp) % pla...]
    ppermute x0 -> x7, waiting for transfers between devices: none -> 3.13 us  [the longest x4 3.07 us: local(): after = jax.lax.ppermute(after, 'chan', in_order)]
    reduce_scatter x2, waiting for transfers between devices: 34.6 us -> 36.9 us  [local(): lax.psum_scatter(stack_term(jnp.int32(0), share_rows * lax.axis_size('win...]
    another operation x1, other arithmetic: 17 us -> 18.2 us
  transfers between devices with their start and end apart: 2 -> 9, of which waited for: 2 -> 5; matrix products, arithmetic and copies ran while one was open for 6% -> 29% of each run, Pallas kernels for 0% -> 0%
where the time goes in v1:
time: 109 us
  waiting for transfers between devices  40.1 us (37%)
  other arithmetic  29.8 us (27%)
  between operations  13.8 us (13%)
  local copies, waits for them, and re-layouts  9.89 us (9%)
  starting transfers between devices  8.72 us (8%)
  matrix products  6.77 us (6%)
    reduce_scatter x2, waiting for transfers between devices, local(): lax.psum_scatter(stack_term(jnp.int32(0), share_rows * lax.axis_size('win...  36.9 us
    another operation x1, other arithmetic  18.2 us
    ppermute x3, starting transfers between devices, local(): latest = jax.lax.ppermute(latest, 'chan', blocks_here)  8.16 us
    dot_general x2, matrix products, cross_block(): jnp.dot(cross_both.reshape(-1, 2 * half_width), trig_table, preferred_ele...  6.77 us
    dynamic_update_slice x4, local copies, waits for them, and re-layouts, local(): lax.dynamic_update_slice_in_dim(everything, after, (carry_out - pp) % pla...  4.07 us
    convert_element_type x1, other arithmetic, cross_block(): (src_real * rec_real + src_imag * rec_imag).astype(jnp.bfloat16)  3.59 us
    ppermute x4, waiting for transfers between devices, local(): after = jax.lax.ppermute(after, 'chan', in_order)  3.07 us
    dynamic_update_slice x3, local copies, waits for them, and re-layouts, local(): lax.dynamic_update_slice_in_dim(everything, latest, (carry_out + pp) % pl...  3.05 us
  transfers between devices with their start and end apart: 9, of which 5 were waited for; matrix products, arithmetic and copies ran while one was open for 29% of the time, Pallas kernels for 0%

profile of v1, /device:TPU:0, one launch (start us, length us, event | category | flops | bytes accessed | tf_op | source)
XLA Modules:
  0.0 109.0 jit_solution(11735645967822483)
XLA Ops:
  6.5 0.9 fusion.21
  7.4 1.9 %multiply_reduce_fusion = f32[32]{0:T(128)S(1)} fusion(f32[1,32,2,4096]{3,2,1,0:T(2,128)} %param.3), kind=kLoop, calls=%fused_computation.25 | loop fusion | flops 524256 | bytes 1048704 | tf_op jit(solution)/shard_map/reduce_sum | solution.py:11
  9.3 0.7 convert_bitcast_fusion
  10.0 1.9 %fusion.12 = bf16[1,32,2,4096]{3,2,1,0:T(2,128)(2,1)S(1)} fusion(f32[1,32,2,4096]{3,2,1,0:T(2,128)} %param.3, f32[32]{0:T(128)S(1)} %add_sqrt_fusion, f32[32]{0:T(128)S(1)} %convert_bitcast_fusion), kind=kLoop, calls=%fused_computation.27 | loop fusion | flops 786432 | bytes 1573120 | tf_op jit(solution)/shard_map/convert_element_type | solution.py:14
  11.9 0.3 copy.12
  12.2 0.1 and_reduce_fusion
  12.3 0.6 gather_fusion
  12.9 0.1 broadcast_select_fusion
  13.0 0.5 collective-permute-start
  13.5 2.9 %collective-permute-start.1 = (bf16[1,2,1,8192]{3,1,2,0:T(2,128)(2,1)S(1)}, bf16[1,2,1,8192]{3,1,2,0:T(2,128)(2,1)S(1)}, u32[]{:S(2)}, u32[]{:S(2)}) collective-permute-start(bf16[1,2,1,8192]{3,1,2,0:T(2,128)(2,1)S(1)} %broadcast_select_fusion), channel_id=1, source_target_pairs={{0,28},{4,0},{8,4},{12,8},{16,12},{20,16},{24,20},{28,24},{1,29},{... | collective-permute-start | bytes 98312 | tf_op jit(solution)/shard_map/ppermute | solution.py:86
  16.4 1.5 %collective-permute-done = bf16[1,2,1,8192]{3,1,2,0:T(2,128)(2,1)S(1)} collective-permute-done((bf16[1,2,1,8192]{3,1,2,0:T(2,128)(2,1)S(1)}, bf16[1,2,1,8192]{3,1,2,0:T(2,128)(2,1)S(1)}, u32[]{:S(2)}, u32[]{:S(2)}) %collective-permute-start) | collective-permute-done | bytes 32800 | tf_op jit(solution)/shard_map/ppermute | solution.py:78
  18.0 0.0 collective-permute-start.2
  18.0 0.1 collective-permute-done.1
  18.0 2.6 %collective-permute-start.3 = (bf16[1,2,1,8192]{3,1,2,0:T(2,128)(2,1)S(1)}, bf16[1,2,1,8192]{3,1,2,0:T(2,128)(2,1)S(1)}, u32[]{:S(2)}, u32[]{:S(2)}) collective-permute-start(bf16[1,2,1,8192]{3,1,2,0:T(2,128)(2,1)S(1)} %collective-permute-done.1), channel_id=1, source_target_pairs={{0,28},{4,0},{8,4},{12,8},{16,12},{20,16},{24,20},{28,24},{1,29},{... | collective-permute-start | bytes 98312 | tf_op jit(solution)/shard_map/ppermute | solution.py:86
  20.7 1.5 %collective-permute-done.2 = bf16[1,2,1,8192]{3,1,2,0:T(2,128)(2,1)S(1)} collective-permute-done((bf16[1,2,1,8192]{3,1,2,0:T(2,128)(2,1)S(1)}, bf16[1,2,1,8192]{3,1,2,0:T(2,128)(2,1)S(1)}, u32[]{:S(2)}, u32[]{:S(2)}) %collective-permute-start.2) | collective-permute-done | bytes 32800 | tf_op jit(solution)/shard_map/ppermute | solution.py:78
  22.2 0.0 collective-permute-start.4
  22.2 18.2 %cosine_convert_fusion = (bf16[4096,256]{1,0:T(8,128)(2,1)}, bf16[4096,256]{1,0:T(8,128)(2,1)}) fusion(s32[256]{0:T(256)S(1)} %iota_add_fusion), kind=kLoop, calls=%fused_computation.19 | loop fusion | flops 17825792 | bytes 4195328 | tf_op jit(solution)/shard_map/convert.6
  40.4 0.4 reshape.261
  40.8 0.0 collective-permute-done.3
  40.8 2.6 %collective-permute-start.5 = (bf16[1,2,1,8192]{3,1,2,0:T(2,128)(2,1)S(1)}, bf16[1,2,1,8192]{3,1,2,0:T(2,128)(2,1)S(1)}, u32[]{:S(2)}, u32[]{:S(2)}) collective-permute-start(bf16[1,2,1,8192]{3,1,2,0:T(2,128)(2,1)S(1)} %collective-permute-done.3), channel_id=1, source_target_pairs={{0,28},{4,0},{8,4},{12,8},{16,12},{20,16},{24,20},{28,24},{1,29},{... | collective-permute-start | bytes 98312 | tf_op jit(solution)/shard_map/ppermute | solution.py:86
  43.4 0.1 fusion.14
  43.5 0.1 copy.4
  43.7 1.0 dynamic_update_slice.29
  44.8 0.1 copy.5
  44.8 1.0 dynamic_update_slice.30
  45.9 0.1 copy.6
  45.9 1.0 dynamic_update_slice.31
  46.9 0.1 copy.7
  47.0 1.0 dynamic_update_slice.32
  48.0 0.1 copy.8
  48.1 1.0 dynamic_update_slice.33
  49.1 0.1 copy.9
  49.2 1.0 dynamic_update_slice.34
  50.2 0.1 copy.10
  50.3 1.0 dynamic_update_slice.35
  51.3 0.1 copy.11
  51.4 1.0 dynamic_update_slice.36
  52.5 3.6 %add_convert_fusion.1 = (bf16[1,8,32,4096]{3,2,1,0:T(8,128)(2,1)S(1)}, bf16[1,8,32,4096]{3,2,1,0:T(8,128)(2,1)S(1)}, bf16[1,8,32,4096]{3,2,1,0:T(8,128)(2,1)S(1)}, bf16[1,8,32,4096]{3,2,1,0:T(8,128)(2,1)}) fusion(f32[32,4096]{1,0:T(8,128)S(1)} %get-tuple-element.44, f32[8,4096]{1,0:T(8,128)S(1)} %get-tuple-element.53, f32[32,4096]{1,0:T(8,128)S(1)} %get-tuple-element.42, ...), kind=kLoop, calls=%fused_computation.23 | loop fusion | flops 16777216 | bytes 9961472 | tf_op jit(solution)/shard_map/while/body/eval_jaxpr/convert_element_type | solution.py:33
  56.1 2.0 %fusion.3 = f32[8,32,256]{2,1,0:T(8,128)} fusion(bf16[1,8,32,4096]{3,2,1,0:T(8,128)(2,1)S(1)} %get-tuple-element.31, bf16[1,8,32,4096]{3,2,1,0:T(8,128)(2,1)S(1)} %get-tuple-element.30, bf16[4096,256]{1,0:T(8,128)(2,1)S(1)} %copy-done.1, bf16[4096,256]{1,0:T(8,128)(2,1)S(1)} %copy-done), kind=kOutput, calls=%fused_computation.8 | convolution fusion | flops 1090519040 | bytes 8650752 | tf_op jit(solution)/shard_map/while/body/eval_jaxpr/dot_general | solution.py:36
  58.1 0.0 reduce-scatter.3.cloned.1.call-update
  58.1 0.0 reduce-scatter.5.cloned.1.call-start
  58.1 4.8 %fusion.6 = f32[8,32,256]{2,1,0:T(8,128)} fusion(bf16[1,8,32,4096]{3,2,1,0:T(8,128)(2,1)S(1)} %get-tuple-element.34, bf16[1,8,32,4096]{3,2,1,0:T(8,128)(2,1)} %get-tuple-element.40, bf16[4096,256]{1,0:T(8,128)(2,1)} %get-tuple-element.52, bf16[4096,256]{1,0:T(8,128)(2,1)} %get-tuple-element.51), kind=kOutput, calls=%fused_computation.13 | convolution fusion | flops 1090519040 | bytes 8650752 | tf_op jit(solution)/shard_map/while/body/eval_jaxpr/dot_general | solution.py:36
  62.9 0.0 reduce-scatter.5.cloned.1.call-update
  62.9 17.4 %reduce-scatter.3.cloned.1.call-done = f32[2,32,256]{2,1,0:T(8,128)} async-done(((f32[8,32,256]{2,1,0:T(8,128)}), f32[2,32,256]{2,1,0:T(8,128)}) %reduce-scatter.3.cloned.1.call-update) | async-done | bytes 65552 | tf_op jit(solution)/shard_map/reduce_scatter | solution.py:106
  80.4 0.8 multiply_bitcast_fusion.1
  81.2 19.5 %reduce-scatter.5.cloned.1.call-done = f32[2,32,256]{2,1,0:T(8,128)} async-done(((f32[8,32,256]{2,1,0:T(8,128)}), f32[2,32,256]{2,1,0:T(8,128)}) %reduce-scatter.5.cloned.1.call-update) | async-done | bytes 65552 | tf_op jit(solution)/shard_map/reduce_scatter | solution.py:106
  100.7 0.8 multiply_bitcast_fusion
  101.5 0.7 pad_maximum_fusion
  (15 shorter events, 0.1 us)
Async XLA Ops:
  6.5 73.9 %reduce-scatter.3.cloned.1.call-start = ((), (), s32[]{:S(2)}) async-start(), calls=%async_computation.2 | async-start | bytes 327680 | tf_op jit(solution)/shard_map/reduce_scatter | solution.py:106
  13.0 5.0 %collective-permute-start = (bf16[1,2,1,8192]{3,1,2,0:T(2,128)(2,1)S(1)}, bf16[1,2,1,8192]{3,1,2,0:T(2,128)(2,1)S(1)}, u32[]{:S(2)}, u32[]{:S(2)}) collective-permute-start(bf16[1,2,1,8192]{3,1,2,0:T(2,128)(2,1)S(1)} %broadcast_select_fusion), channel_id=1, source_target_pairs={{0,4},{4,8},{8,12},{12,16},{16,20},{20,24},{24,28},{28,0},{1,5},{5... | collective-permute-start | bytes 98312 | tf_op jit(solution)/shard_map/ppermute | solution.py:78
  13.5 4.5 %collective-permute-start.1 = (bf16[1,2,1,8192]{3,1,2,0:T(2,128)(2,1)S(1)}, bf16[1,2,1,8192]{3,1,2,0:T(2,128)(2,1)S(1)}, u32[]{:S(2)}, u32[]{:S(2)}) collective-permute-start(bf16[1,2,1,8192]{3,1,2,0:T(2,128)(2,1)S(1)} %broadcast_select_fusion), channel_id=1, source_target_pairs={{0,28},{4,0},{8,4},{12,8},{16,12},{20,16},{24,20},{28,24},{1,29},{... | collective-permute-start | bytes 98312 | tf_op jit(solution)/shard_map/ppermute | solution.py:86
  18.0 4.2 %collective-permute-start.2 = (bf16[1,2,1,8192]{3,1,2,0:T(2,128)(2,1)S(1)}, bf16[1,2,1,8192]{3,1,2,0:T(2,128)(2,1)S(1)}, u32[]{:S(2)}, u32[]{:S(2)}) collective-permute-start(bf16[1,2,1,8192]{3,1,2,0:T(2,128)(2,1)S(1)} %collective-permute-done), channel_id=1, source_target_pairs={{0,4},{4,8},{8,12},{12,16},{16,20},{20,24},{24,28},{28,0},{1,5},{5... | collective-permute-start | bytes 98312 | tf_op jit(solution)/shard_map/ppermute | solution.py:78
  18.0 22.8 %collective-permute-start.3 = (bf16[1,2,1,8192]{3,1,2,0:T(2,128)(2,1)S(1)}, bf16[1,2,1,8192]{3,1,2,0:T(2,128)(2,1)S(1)}, u32[]{:S(2)}, u32[]{:S(2)}) collective-permute-start(bf16[1,2,1,8192]{3,1,2,0:T(2,128)(2,1)S(1)} %collective-permute-done.1), channel_id=1, source_target_pairs={{0,28},{4,0},{8,4},{12,8},{16,12},{20,16},{24,20},{28,24},{1,29},{... | collective-permute-start | bytes 98312 | tf_op jit(solution)/shard_map/ppermute | solution.py:86
  22.2 21.2 %collective-permute-start.4 = (bf16[1,2,1,8192]{3,1,2,0:T(2,128)(2,1)S(1)}, bf16[1,2,1,8192]{3,1,2,0:T(2,128)(2,1)S(1)}, u32[]{:S(2)}, u32[]{:S(2)}) collective-permute-start(bf16[1,2,1,8192]{3,1,2,0:T(2,128)(2,1)S(1)} %collective-permute-done.2), channel_id=1, source_target_pairs={{0,4},{4,8},{8,12},{12,16},{16,20},{20,24},{24,28},{28,0},{1,5},{5... | collective-permute-start | bytes 98312 | tf_op jit(solution)/shard_map/ppermute | solution.py:78
  40.8 9.4 %collective-permute-start.5 = (bf16[1,2,1,8192]{3,1,2,0:T(2,128)(2,1)S(1)}, bf16[1,2,1,8192]{3,1,2,0:T(2,128)(2,1)S(1)}, u32[]{:S(2)}, u32[]{:S(2)}) collective-permute-start(bf16[1,2,1,8192]{3,1,2,0:T(2,128)(2,1)S(1)} %collective-permute-done.3), channel_id=1, source_target_pairs={{0,28},{4,0},{8,4},{12,8},{16,12},{20,16},{24,20},{28,24},{1,29},{... | collective-permute-start | bytes 98312 | tf_op jit(solution)/shard_map/ppermute | solution.py:86
  43.4 7.9 %collective-permute-start.6 = (bf16[1,2,1,8192]{3,1,2,0:T(2,128)(2,1)S(1)}, bf16[1,2,1,8192]{3,1,2,0:T(2,128)(2,1)S(1)}, u32[]{:S(2)}, u32[]{:S(2)}) collective-permute-start(bf16[1,2,1,8192]{3,1,2,0:T(2,128)(2,1)S(1)} %collective-permute-done.4), channel_id=1, source_target_pairs={{0,4},{4,8},{8,12},{12,16},{16,20},{20,24},{24,28},{28,0},{1,5},{5... | collective-permute-start | bytes 98312 | tf_op jit(solution)/shard_map/ppermute | solution.py:78
  52.5 3.6 %copy-start = (bf16[4096,256]{1,0:T(8,128)(2,1)S(1)}, bf16[4096,256]{1,0:T(8,128)(2,1)}, u32[]{:S(2)}) copy-start(bf16[4096,256]{1,0:T(8,128)(2,1)} %get-tuple-element.51) | copy-start | bytes 6291460
  52.5 3.6 %copy-start.1 = (bf16[4096,256]{1,0:T(8,128)(2,1)S(1)}, bf16[4096,256]{1,0:T(8,128)(2,1)}, u32[]{:S(2)}) copy-start(bf16[4096,256]{1,0:T(8,128)(2,1)} %get-tuple-element.52) | copy-start | bytes 6291460
  58.1 42.6 %reduce-scatter.5.cloned.1.call-start = ((), (), s32[]{:S(2)}) async-start(), calls=%async_computation.3 | async-start | bytes 327680 | tf_op jit(solution)/shard_map/reduce_scatter | solution.py:106
Sparse Core Ops, SparseCore 0:
  58.2 22.1 reduce-scatter.2
  82.7 17.9 reduce-scatter.4
